TPU v7x, 32 devices: a whole 2x2x4 slice. The times are simulated.
32 devices in a mesh: gx: 16 (over z, x, core), gy: 2 (over y).
Axes of the slice: x: 2, y: 2, z: 4, core: 2. Of those that a mesh axis runs over, the one named last changes fastest.
Arguments:
- potential: float32 [3, 1, 4096, 256], P(None, None, 'gx', 'gy'), may hold values from -8 to 8
- labels: int32 [1, 4096, 256], P(None, 'gx', 'gy'), may hold values from 0 to 7
- principal: float32 [2, 8], replicated, may hold values from 0.5 to 16
- off_diagonal: float32 [3, 8], replicated, may hold values from -0.4 to 0.4
Outputs:
- updated: float32 [3, 1, 4096, 256], P(None, None, 'gx', 'gy')
All inputs are finite; a program needn't handle non-finite values.
Results may differ from a plain program's by a relative error of at most 0.0017.
Values sent between devices are 32-bit elements; how exact they have to be, the bound alone decides.
A program may use at most 64 MiB of HBM per device.

v0:
```python
import jax
import jax.numpy as jnp
from jax import lax
from jax.sharding import PartitionSpec as P


def shifted_2(shard, axis, by):
    size = lax.axis_size(axis)
    return lax.ppermute(shard, axis, [(i, (i + by) % size) for i in range(size)])


def padded_2(cells, sides, width):
    for axis, dim in sides:
        count = lax.axis_size(axis)
        head = lax.slice_in_dim(cells, 0, width, axis=dim)
        tail = lax.slice_in_dim(cells, cells.shape[dim] - width, cells.shape[dim], axis=dim)
        cells = jnp.concatenate(
            [
                lax.ppermute(tail, axis, [(i, (i + 1) % count) for i in range(count)]),
                cells,
                lax.ppermute(head, axis, [((i + 1) % count, i) for i in range(count)]),
            ],
            axis=dim,
        )
    return cells


def harmonic(first, second):
    return 2.0 * first * second / (first + second)


def neighbour(values, offset, axis_dim, filler):
    extent = values.shape[axis_dim]
    dims_pad = list(values.shape)
    dims_pad[axis_dim] = abs(offset)
    padding = jnp.full(tuple(dims_pad), filler, values.dtype)
    if offset > 0:
        retained = lax.slice_in_dim(values, 0, extent - offset, axis=axis_dim)
        return jnp.concatenate([padding, retained], axis_dim)
    retained = lax.slice_in_dim(values, -offset, extent, axis=axis_dim)
    return jnp.concatenate([retained, padding], axis_dim)


def shifted(values, offset, axis_dim, wrap, filler):
    if wrap:
        return jnp.roll(values, offset, axis_dim)
    return neighbour(values, offset, axis_dim, filler)


def cyclic_reduce(sub_diag, main_diag, super_diag, forcing, axis_dim, wrap):
    extent = sub_diag.shape[axis_dim]
    stride = 1
    while stride < extent:
        low_before = shifted(sub_diag, stride, axis_dim, wrap, 0.0)
        main_before = shifted(main_diag, stride, axis_dim, wrap, 1.0)
        high_before = shifted(super_diag, stride, axis_dim, wrap, 0.0)
        rest_before = shifted(forcing, stride, axis_dim + 1, wrap, 0.0)
        low_after = shifted(sub_diag, -stride, axis_dim, wrap, 0.0)
        main_after = shifted(main_diag, -stride, axis_dim, wrap, 1.0)
        high_after = shifted(super_diag, -stride, axis_dim, wrap, 0.0)
        rest_after = shifted(forcing, -stride, axis_dim + 1, wrap, 0.0)
        factor_low = -sub_diag / main_before
        factor_high = -super_diag / main_after
        forcing = forcing + factor_low[None] * rest_before + factor_high[None] * rest_after
        main_diag = main_diag + factor_low * high_before + factor_high * low_after
        sub_diag = factor_low * low_before
        super_diag = factor_high * high_after
        stride = stride * 2
    return forcing / (sub_diag + main_diag + super_diag)[None]


def reduced_rows(tail_row, next_head, low_last, main_last, high_last, force_last):
    reduced_low = -low_last * tail_row[3]
    reduced_main = main_last - low_last * tail_row[4] - high_last * next_head[3]
    reduced_high = -high_last * next_head[4]
    reduced_force = force_last - low_last[None] * tail_row[:3] - high_last[None] * next_head[:3]
    return jnp.concatenate(
        [reduced_low[None], reduced_main[None], reduced_high[None], reduced_force], 0
    )


def spike_solve(sub_diag, main_diag, super_diag, forcing, axis_dim, interface):
    length = sub_diag.shape[axis_dim]
    position = lax.broadcasted_iota(jnp.int32, sub_diag.shape, axis_dim)
    is_last = position == length - 1
    low_inner = jnp.where((position == 0) | is_last, 0.0, sub_diag)
    high_inner = jnp.where((position == length - 2) | is_last, 0.0, super_diag)
    main_inner = jnp.where(is_last, 1.0, main_diag)
    left_spike = jnp.where(position == 0, sub_diag, 0.0)
    right_spike = jnp.where(position == length - 2, super_diag, 0.0)
    stacked = jnp.concatenate(
        [jnp.where(is_last[None], 0.0, forcing), left_spike[None], right_spike[None]], 0
    )
    solved = cyclic_reduce(low_inner, main_inner, high_inner, stacked, axis_dim, False)
    head_row = lax.slice_in_dim(solved, 0, 1, axis=axis_dim + 1)
    tail_row = lax.slice_in_dim(solved, length - 2, length - 1, axis=axis_dim + 1)
    low_last = lax.slice_in_dim(sub_diag, length - 1, length, axis=axis_dim)
    main_last = lax.slice_in_dim(main_diag, length - 1, length, axis=axis_dim)
    high_last = lax.slice_in_dim(super_diag, length - 1, length, axis=axis_dim)
    force_last = lax.slice_in_dim(forcing, length - 1, length, axis=axis_dim + 1)
    own_value, prev_value = interface(
        head_row, tail_row, low_last, main_last, high_last, force_last
    )
    inner_values = solved[:3] - solved[3][None] * prev_value - solved[4][None] * own_value
    return jnp.where(is_last[None], own_value, inner_values)


def pick_values(solution, members, my_index, axis_dim):
    own_value = lax.dynamic_slice_in_dim(solution, my_index, 1, axis_dim)
    prev_value = lax.dynamic_slice_in_dim(solution, (my_index + members - 1) % members, 1, axis_dim)
    return (own_value, prev_value)


def interface_x(head_row, tail_row, low_last, main_last, high_last, force_last):
    members = lax.axis_size("gx")
    my_index = lax.axis_index("gx")
    next_head = shifted_2(head_row, "gx", -1)
    rows_here = reduced_rows(tail_row, next_head, low_last, main_last, high_last, force_last)
    gathered = lax.all_gather(rows_here, "gx", axis=2, tiled=True)
    solution = cyclic_reduce(gathered[0], gathered[1], gathered[2], gathered[3:], 1, True)
    return pick_values(solution, members, my_index, 2)


def interface_y(head_row, tail_row, low_last, main_last, high_last, force_last):
    members = lax.axis_size("gy")
    next_head = shifted_2(head_row, "gy", -1)
    rows_here = reduced_rows(tail_row, next_head, low_last, main_last, high_last, force_last)
    gathered = lax.all_gather(rows_here, "gy", axis=3, tiled=True)
    solution = cyclic_reduce(gathered[0], gathered[1], gathered[2], gathered[3:], 2, True)
    return pick_values(solution, members, lax.axis_index("gy"), 3)


def lookup_phase(components, label_block):
    cell_tensor = jnp.zeros((5,) + label_block.shape, jnp.float32)
    for phase_id in range(components.shape[1]):
        cell_tensor = jnp.where(
            (label_block == phase_id)[None],
            components[:, phase_id][:, None, None, None],
            cell_tensor,
        )
    return cell_tensor


def local(potential, labels, principal, off_diagonal):
    components = jnp.concatenate([principal, off_diagonal], 0)
    cell_tensor = lookup_phase(components, labels)
    padded = padded_2(cell_tensor, (("gx", 2), ("gy", 3)), 1)
    damping = 2.0 / (potential.shape[3] * potential.shape[3])
    along_xdir = padded[:, :, :, 1:-1]
    cond_xx = along_xdir[0]
    face_east = harmonic(cond_xx[:, 1:-1], cond_xx[:, 2:])
    face_west = harmonic(cond_xx[:, :-2], cond_xx[:, 1:-1])
    source_x = jnp.stack(
        [
            face_east - face_west,
            0.5 * (along_xdir[2][:, 2:] - along_xdir[2][:, :-2]),
            0.5 * (along_xdir[3][:, 2:] - along_xdir[3][:, :-2]),
        ]
    )
    half_step = spike_solve(
        -face_west,
        damping + face_west + face_east,
        -face_east,
        damping * potential + source_x,
        1,
        interface_x,
    )
    along_ydir = padded[:, :, 1:-1, :]
    cond_yy = along_ydir[1]
    face_north = harmonic(cond_yy[:, :, 1:-1], cond_yy[:, :, 2:])
    face_south = harmonic(cond_yy[:, :, :-2], cond_yy[:, :, 1:-1])
    source_y = jnp.stack(
        [
            0.5 * (along_ydir[2][:, :, 2:] - along_ydir[2][:, :, :-2]),
            face_north - face_south,
            0.5 * (along_ydir[4][:, :, 2:] - along_ydir[4][:, :, :-2]),
        ]
    )
    return spike_solve(
        -face_south,
        damping + face_south + face_north,
        -face_north,
        damping * half_step + source_y,
        2,
        interface_y,
    )


def solution(mesh):
    in_specs = (P(None, None, "gx", "gy"), P(None, "gx", "gy"), P(), P())
    out_specs = P(None, None, "gx", "gy")
    return jax.shard_map(local, mesh=mesh, in_specs=in_specs, out_specs=out_specs, check_vma=False)
```

profile of v0, /device:TPU:0, one launch (start us, length us, event | category | flops | bytes accessed | tf_op | source)
XLA Modules:
  0.0 70.5 jit_solution(12789829236502406646)
XLA Ops:
  0.0 0.7 pad_maximum_fusion.15
  0.7 0.3 slice_reduce_fusion.9
  1.0 1.1 %compare_bitcast_fusion.7 = (pred[256,128]{1,0:T(8,128)(4,1)S(1)}, pred[256,128]{1,0:T(8,128)(4,1)S(1)}, pred[256,128]{1,0:T(8,128)(4,1)S(1)}, pred[256,128]{1,0...) fusion(s32[1,256,128]{2,1,0:T(8,128)} %param.5), kind=kLoop, calls=%fused_computation.147 | loop fusion | flops 262144 | bytes 393216 | tf_op jit(solution)/shard_map/jit(_where)/broadcast_in_dim | solution.py:136
  3.1 0.3 select_select_fusion
  3.6 5.5 %collective-permute-start.1 = (f32[5,1,1,128]{2,3,1,0:T(8,128)S(1)}, f32[5,1,1,128]{2,3,1,0:T(8,128)S(1)}, u32[]{:S(2)}, u32[]{:S(2)}) collective-permute-start(f32[5,1,1,128]{2,3,1,0:T(8,128)S(1)} %get-tuple-element.150), channel_id=1, source_target_pairs={{2,0},{4,2},{6,4},{8,6},{10,8},{12,10},{14,12},{16,14},{18,16},{20... | collective-permute-start | bytes 7688 | tf_op jit(solution)/shard_map/ppermute | solution.py:21
  9.0 0.6 iota_compare_fusion.5
  9.6 0.6 fusion.77
  10.2 0.5 iota_compare_fusion.4
  10.7 0.5 iota_compare_fusion.3
  11.2 0.6 fusion.76
  12.1 1.6 %collective-permute-done.1 = f32[5,1,1,128]{2,3,1,0:T(8,128)S(1)} collective-permute-done((f32[5,1,1,128]{2,3,1,0:T(8,128)S(1)}, f32[5,1,1,128]{2,3,1,0:T(8,128)S(1)}, u32[]{:S(2)}, u32[]{:S(2)}) %collective-permute-start.1) | collective-permute-done | bytes 2592 | tf_op jit(solution)/shard_map/ppermute | solution.py:21
  13.6 4.6 %collective-permute-done = f32[5,1,1,128]{2,3,1,0:T(8,128)S(1)} collective-permute-done((f32[5,1,1,128]{2,3,1,0:T(8,128)S(1)}, f32[5,1,1,128]{2,3,1,0:T(8,128)S(1)}, u32[]{:S(2)}, u32[]{:S(2)}) %collective-permute-start) | collective-permute-done | bytes 2592 | tf_op jit(solution)/shard_map/ppermute | solution.py:19
  18.7 0.7 broadcast_select_fusion.3
  20.1 0.3 multiply_add_fusion.12
  21.4 0.3 multiply_add_fusion.11
  22.6 0.3 multiply_add_fusion.10
  28.8 0.7 %pad_maximum_fusion.13 = (f32[5,1,258,1]{2,3,1,0:T(1,128)}, f32[5,1,258,1]{2,3,1,0:T(1,128)}) fusion(f32[5,1,1,128]{2,3,1,0:T(8,128)S(1)} %collective-permute-done.1, f32[5,1,256,128]{2,3,1,0:T(8,128)S(1)} %select_select_fusion, f32[5,1,1,128]{2,3,1,0:T(8,128)S(1)} %collective-permute-done), kind=kLoop, calls=%fused_computation.248 | loop fusion | flops 5160 | bytes 670800 | tf_op jit(solution)/shard_map/slice | solution.py:16
  29.6 1.6 %collective-permute-start.3 = (f32[5,1,258,1]{2,3,1,0:T(1,128)}, f32[5,1,258,1]{2,3,1,0:T(1,128)S(1)}, u32[]{:S(2)}, u32[]{:S(2)}) collective-permute-start(f32[5,1,258,1]{2,3,1,0:T(1,128)} %get-tuple-element.112), channel_id=1, source_target_pairs={{1,0},{0,1},{3,2},{2,3},{5,4},{4,5},{7,6},{6,7},{9,8},{8,9},{11,10... | collective-permute-start | bytes 15488 | tf_op jit(solution)/shard_map/ppermute | solution.py:21
  31.2 0.5 collective-permute-start.2
  31.8 0.6 copy.142
  32.5 0.8 %collective-permute-done.4 = f32[5,1,1,128]{2,3,1,0:T(8,128)S(1)} collective-permute-done((f32[5,1,1,128]{2,3,1,0:T(8,128)S(1)}, f32[5,1,1,128]{2,3,1,0:T(8,128)S(1)}, u32[]{:S(2)}, u32[]{:S(2)}) %collective-permute-start.4) | collective-permute-done | bytes 2592 | tf_op jit(solution)/shard_map/ppermute | solution.py:9
  33.5 0.8 %copy-done.1 = f32[1,256,128]{1,2,0:T(8,128)S(1)} copy-done((f32[1,256,128]{1,2,0:T(8,128)S(1)}, f32[1,256,128]{1,2,0:T(8,128)}, u32[]{:S(2)}) %copy-start.1) | copy-done | bytes 131096
  34.3 0.3 fusion.24
  34.6 0.6 copy-done.2
  35.2 18.7 %all_gather.6 = f32[6,1,16,128]{3,1,0,2:T(1,128)S(1)} all-gather(f32[6,1,1,128]{3,1,0,2:T(1,128)S(1)} %maximum_bitcast_fusion.5), channel_id=1, replica_groups=mesh['gx'=16,'gy'=2] {'gx'}, dimensions={2}, use_global_device_ids=true | all-gather | bytes 52224 | tf_op jit(solution)/shard_map/all_gather | solution.py:119
  55.2 0.7 copy-done.3
  56.0 0.6 copy-done.9
  56.8 0.7 copy-done.5
  61.2 1.6 %collective-permute-start.5 = (f32[5,1,256,1]{2,3,1,0:T(1,128)S(1)}, f32[5,1,256,1]{2,3,1,0:T(1,128)S(1)}, u32[]{:S(2)}, u32[]{:S(2)}) collective-permute-start(f32[5,1,256,1]{2,3,1,0:T(1,128)S(1)} %slice.1303), channel_id=1, source_target_pairs={{0,1},{1,0},{2,3},{3,2},{4,5},{5,4},{6,7},{7,6},{8,9},{9,8},{10,11... | collective-permute-start | bytes 15368 | tf_op jit(solution)/shard_map/ppermute | solution.py:9
  62.8 2.1 %collective-permute-done.5 = f32[5,1,256,1]{2,3,1,0:T(1,128)S(1)} collective-permute-done((f32[5,1,256,1]{2,3,1,0:T(1,128)S(1)}, f32[5,1,256,1]{2,3,1,0:T(1,128)S(1)}, u32[]{:S(2)}, u32[]{:S(2)}) %collective-permute-start.5) | collective-permute-done | bytes 5152 | tf_op jit(solution)/shard_map/ppermute | solution.py:9
  65.0 4.4 %all_gather.7 = f32[6,1,256,2]{2,1,0,3:T(1,128)S(1)} all-gather(f32[6,1,256,1]{2,1,0,3:T(1,128)S(1)} %maximum_bitcast_fusion.4), channel_id=1, replica_groups=mesh['gx'=16,'gy'=2] {'gy'}, dimensions={3}, use_global_device_ids=true | all-gather | bytes 18432 | tf_op jit(solution)/shard_map/all_gather | solution.py:128
  69.6 0.9 %copy.153 = f32[3,1,256,128]{3,2,1,0:T(8,128)} copy(f32[3,1,256,128]{2,3,1,0:T(8,128)S(1)} %fusion.1) | data formatting | bytes 786432 | tf_op jit(solution)/shard_map/jit(_where)/select_n | solution.py:105
  (229 shorter events, 15.1 us)
Async XLA Ops:
  3.4 8.5 %copy-start = (f32[3,1,256,128]{3,2,1,0:T(8,128)S(1)}, f32[3,1,256,128]{3,2,1,0:T(8,128)}, u32[]{:S(2)}) copy-start(f32[3,1,256,128]{3,2,1,0:T(8,128)} %param.4) | copy-start | bytes 1179652
  3.6 10.1 %collective-permute-start.1 = (f32[5,1,1,128]{2,3,1,0:T(8,128)S(1)}, f32[5,1,1,128]{2,3,1,0:T(8,128)S(1)}, u32[]{:S(2)}, u32[]{:S(2)}) collective-permute-start(f32[5,1,1,128]{2,3,1,0:T(8,128)S(1)} %get-tuple-element.150), channel_id=1, source_target_pairs={{2,0},{4,2},{6,4},{8,6},{10,8},{12,10},{14,12},{16,14},{18,16},{20... | collective-permute-start | bytes 7688 | tf_op jit(solution)/shard_map/ppermute | solution.py:21
  9.0 9.2 %collective-permute-start = (f32[5,1,1,128]{2,3,1,0:T(8,128)S(1)}, f32[5,1,1,128]{2,3,1,0:T(8,128)S(1)}, u32[]{:S(2)}, u32[]{:S(2)}) collective-permute-start(f32[5,1,1,128]{2,3,1,0:T(8,128)S(1)} %get-tuple-element.149), channel_id=1, source_target_pairs={{0,2},{2,4},{4,6},{6,8},{8,10},{10,12},{12,14},{14,16},{16,18},{18... | collective-permute-start | bytes 7688 | tf_op jit(solution)/shard_map/ppermute | solution.py:19
  11.8 7.9 %copy-start.4 = (pred[256]{0:T(512)(128)(4,1)}, pred[256]{0:T(512)(128)(4,1)S(1)}, u32[]{:S(2)}) copy-start(pred[256]{0:T(512)(128)(4,1)S(1)} %iota_compare_fusion.2) | copy-start | bytes 772
  28.6 4.8 %collective-permute-start.4 = (f32[5,1,1,128]{2,3,1,0:T(8,128)S(1)}, f32[5,1,1,128]{2,3,1,0:T(8,128)S(1)}, u32[]{:S(2)}, u32[]{:S(2)}) collective-permute-start(f32[5,1,1,128]{2,3,1,0:T(8,128)S(1)} %slice.1169), channel_id=1, source_target_pairs={{0,30},{2,0},{4,2},{6,4},{8,6},{10,8},{12,10},{14,12},{16,14},{18,... | collective-permute-start | bytes 7688 | tf_op jit(solution)/shard_map/ppermute | solution.py:9
  29.6 25.3 %collective-permute-start.3 = (f32[5,1,258,1]{2,3,1,0:T(1,128)}, f32[5,1,258,1]{2,3,1,0:T(1,128)S(1)}, u32[]{:S(2)}, u32[]{:S(2)}) collective-permute-start(f32[5,1,258,1]{2,3,1,0:T(1,128)} %get-tuple-element.112), channel_id=1, source_target_pairs={{1,0},{0,1},{3,2},{2,3},{5,4},{4,5},{7,6},{6,7},{9,8},{8,9},{11,10... | collective-permute-start | bytes 15488 | tf_op jit(solution)/shard_map/ppermute | solution.py:21
  31.2 23.7 %collective-permute-start.2 = (f32[5,1,258,1]{2,3,1,0:T(1,128)}, f32[5,1,258,1]{2,3,1,0:T(1,128)S(1)}, u32[]{:S(2)}, u32[]{:S(2)}) collective-permute-start(f32[5,1,258,1]{2,3,1,0:T(1,128)} %get-tuple-element.111), channel_id=1, source_target_pairs={{0,1},{1,0},{2,3},{3,2},{4,5},{5,4},{6,7},{7,6},{8,9},{9,8},{10,11... | collective-permute-start | bytes 15488 | tf_op jit(solution)/shard_map/ppermute | solution.py:19
  33.4 0.9 %copy-start.1 = (f32[1,256,128]{1,2,0:T(8,128)S(1)}, f32[1,256,128]{1,2,0:T(8,128)}, u32[]{:S(2)}) copy-start(f32[1,256,128]{1,2,0:T(8,128)} %get-tuple-element.102) | copy-start | bytes 393220
  34.6 0.6 copy-start.2
  55.2 0.7 copy-start.3
  55.9 0.7 copy-start.9
  56.0 0.7 copy-start.6
  56.0 0.7 copy-start.7
  56.0 0.6 copy-start.8
  56.8 0.7 copy-start.5
  61.2 3.7 %collective-permute-start.5 = (f32[5,1,256,1]{2,3,1,0:T(1,128)S(1)}, f32[5,1,256,1]{2,3,1,0:T(1,128)S(1)}, u32[]{:S(2)}, u32[]{:S(2)}) collective-permute-start(f32[5,1,256,1]{2,3,1,0:T(1,128)S(1)} %slice.1303), channel_id=1, source_target_pairs={{0,1},{1,0},{2,3},{3,2},{4,5},{5,4},{6,7},{7,6},{8,9},{9,8},{10,11... | collective-permute-start | bytes 15368 | tf_op jit(solution)/shard_map/ppermute | solution.py:9
where the time goes:
time: 70.8 us; the launch traced here: 70.5 us
  blocking collectives  23.1 us (33%)
  other arithmetic  15.5 us (22%)
  local copies, waits for them, and re-layouts  12 us (17%)
  starting transfers between devices  9.31 us (13%)
  waiting for transfers between devices  9.1 us (13%)
  between operations  1.55 us (2%)
    all_gather x1, blocking collectives, interface_x(): gathered = lax.all_gather(rows_here, 'gx', axis=2, tiled=True)  18.7 us
    ppermute x2, starting transfers between devices, padded_2(): lax.ppermute(head, axis, [((i + 1) % count, i) for i in range(count)])  7.05 us
    ppermute x2, waiting for transfers between devices, padded_2(): lax.ppermute(tail, axis, [(i, (i + 1) % count) for i in range(count)])  4.61 us
    all_gather x1, blocking collectives, interface_y(): gathered = lax.all_gather(rows_here, 'gy', axis=3, tiled=True)  4.36 us
    slice x47, local copies, waits for them, and re-layouts, neighbour(): retained = lax.slice_in_dim(values, 0, extent - offset, axis=axis_dim)  3.91 us
    unnamed x28, local copies, waits for them, and re-layouts  3.57 us
    add x16, other arithmetic, cyclic_reduce(): forcing + factor_low[None] * rest_before + factor_high[None] * rest_after  3.03 us
    ppermute x2, waiting for transfers between devices, shifted_2(): lax.ppermute(shard, axis, [(i, (i + by) % size) for i in range(size)])  2.92 us
  transfers between devices with their start and end apart: 6, of which 4 were waited for; matrix products, arithmetic and copies ran while one was open for 8% of the time, Pallas kernels for 0%

commit v1 on v0

--- a/solution.py
+++ b/solution.py
@@ -2,6 +2,28 @@
 import jax.numpy as jnp
 from jax import lax
 from jax.sharding import PartitionSpec as P
+
+
+def laid_out(blocks, dim):
+    lengths = list(blocks.shape[1:])
+    lengths[dim] *= blocks.shape[0]
+    return jnp.moveaxis(blocks, 0, dim).reshape(lengths)
+
+
+def doubled(x, axis):
+    size = lax.axis_size(axis)
+    parts = x[None]
+    for level in range(size.bit_length() - 1):
+        bit = 1 << level
+        other = lax.ppermute(parts, axis, [(i, i ^ bit) for i in range(size)])
+        both = jnp.stack([parts, other])
+        upper = lax.axis_index(axis) >> level & 1
+        parts = jnp.where(upper == 0, both, both[::-1]).reshape(-1, *x.shape)
+    return parts
+
+
+def gather_by_bits(x, axis, dim):
+    return laid_out(doubled(x, axis), dim)
 
 
 def shifted_2(shard, axis, by):
@@ -116,7 +138,7 @@
     my_index = lax.axis_index("gx")
     next_head = shifted_2(head_row, "gx", -1)
     rows_here = reduced_rows(tail_row, next_head, low_last, main_last, high_last, force_last)
-    gathered = lax.all_gather(rows_here, "gx", axis=2, tiled=True)
+    gathered = gather_by_bits(rows_here, "gx", 2)
     solution = cyclic_reduce(gathered[0], gathered[1], gathered[2], gathered[3:], 1, True)
     return pick_values(solution, members, my_index, 2)
 

time: 70.8 us -> 65.1 us (0.919)
  blocking collectives: 23.1 us -> 4.36 us
  waiting for transfers between devices: 9.1 us -> 18.7 us
  starting transfers between devices: 9.31 us -> 11.9 us
    all_gather x1 -> x0, blocking collectives: 18.7 us -> none  [interface_x(): gathered = lax.all_gather(rows_here, 'gx', axis=2, tiled=True)]
    ppermute x0 -> x4, waiting for transfers between devices: none -> 9.73 us  [doubled(): other = lax.ppermute(parts, axis, [(i, i ^ bit) for i in range(size)])]
    ppermute x0 -> x4, starting transfers between devices: none -> 2.45 us  [doubled(): other = lax.ppermute(parts, axis, [(i, i ^ bit) for i in range(size)])]
    unnamed x28, local copies, waits for them, and re-layouts: 3.57 us -> 4.29 us
    add x13 -> x16, other arithmetic: 1.4 us -> 1.49 us  [cyclic_reduce(): main_diag = main_diag + factor_low * high_before + factor_high * low_after]
    mul x16 -> x15, other arithmetic: 1.79 us -> 1.75 us  [cyclic_reduce(): factor_low[None] * rest_before]
  transfers between devices with their start and end apart: 6 -> 10, of which waited for: 4 -> 7; matrix products, arithmetic and copies ran while one was open for 8% -> 11% of each run, Pallas kernels for 0% -> 0%
where the time goes in v1:
time: 65.1 us; the launch traced here: 64.9 us
  waiting for transfers between devices  18.7 us (29%)
  other arithmetic  15.5 us (24%)
  local copies, waits for them, and re-layouts  12.7 us (20%)
  starting transfers between devices  11.9 us (18%)
  blocking collectives  4.36 us (7%)
  between operations  1.63 us (3%)
    ppermute x4, waiting for transfers between devices, doubled(): other = lax.ppermute(parts, axis, [(i, i ^ bit) for i in range(size)])  9.73 us
    ppermute x2, starting transfers between devices, padded_2(): lax.ppermute(head, axis, [((i + 1) % count, i) for i in range(count)])  7.05 us
    ppermute x2, waiting for transfers between devices, padded_2(): lax.ppermute(tail, axis, [(i, (i + 1) % count) for i in range(count)])  4.61 us
    all_gather x1, blocking collectives, interface_y(): gathered = lax.all_gather(rows_here, 'gy', axis=3, tiled=True)  4.36 us
    unnamed x28, local copies, waits for them, and re-layouts  4.29 us
    slice x47, local copies, waits for them, and re-layouts, neighbour(): retained = lax.slice_in_dim(values, 0, extent - offset, axis=axis_dim)  3.91 us
    add x16, other arithmetic, cyclic_reduce(): forcing + factor_low[None] * rest_before + factor_high[None] * rest_after  2.89 us
    ppermute x2, waiting for transfers between devices, shifted_2(): lax.ppermute(shard, axis, [(i, (i + by) % size) for i in range(size)])  2.86 us
  transfers between devices with their start and end apart: 10, of which 7 were waited for; matrix products, arithmetic and copies ran while one was open for 11% of the time, Pallas kernels for 0%

profile of v1, /device:TPU:0, one launch (start us, length us, event | category | flops | bytes accessed | tf_op | source)
XLA Modules:
  0.0 64.9 jit_solution(12969397049228867971)
XLA Ops:
  0.0 0.7 %pad_maximum_fusion.19 = f32[5,8]{1,0:T(8,128)S(1)} fusion(f32[3,8]{1,0:T(4,128)} %param.7, f32[2,8]{1,0:T(2,128)} %param.6), kind=kLoop, calls=%fused_computation.276 | loop fusion | flops 40 | bytes 320 | tf_op jit(solution)/shard_map/concatenate | solution.py:167
  1.0 1.1 %compare_bitcast_fusion.7 = (pred[256,128]{1,0:T(8,128)(4,1)S(1)}, pred[256,128]{1,0:T(8,128)(4,1)S(1)}, pred[256,128]{1,0:T(8,128)(4,1)S(1)}, pred[256,128]{1,0...) fusion(s32[1,256,128]{2,1,0:T(8,128)} %param.5), kind=kLoop, calls=%fused_computation.147 | loop fusion | flops 262144 | bytes 393216 | tf_op jit(solution)/shard_map/jit(_where)/broadcast_in_dim | solution.py:158
  3.1 0.3 select_select_fusion
  3.6 5.5 %collective-permute-start.1 = (f32[5,1,1,128]{2,3,1,0:T(8,128)S(1)}, f32[5,1,1,128]{2,3,1,0:T(8,128)S(1)}, u32[]{:S(2)}, u32[]{:S(2)}) collective-permute-start(f32[5,1,1,128]{2,3,1,0:T(8,128)S(1)} %get-tuple-element.151), channel_id=1, source_target_pairs={{2,0},{4,2},{6,4},{8,6},{10,8},{12,10},{14,12},{16,14},{18,16},{20... | collective-permute-start | bytes 7688 | tf_op jit(solution)/shard_map/ppermute | solution.py:43
  9.0 0.6 iota_compare_fusion.5
  9.6 0.6 fusion.77
  10.2 0.6 iota_compare_fusion.3
  10.8 0.6 fusion.78
  11.4 0.5 iota_compare_fusion.4
  12.1 1.5 %collective-permute-done.1 = f32[5,1,1,128]{2,3,1,0:T(8,128)S(1)} collective-permute-done((f32[5,1,1,128]{2,3,1,0:T(8,128)S(1)}, f32[5,1,1,128]{2,3,1,0:T(8,128)S(1)}, u32[]{:S(2)}, u32[]{:S(2)}) %collective-permute-start.1) | collective-permute-done | bytes 2592 | tf_op jit(solution)/shard_map/ppermute | solution.py:43
  13.6 4.6 %collective-permute-done = f32[5,1,1,128]{2,3,1,0:T(8,128)S(1)} collective-permute-done((f32[5,1,1,128]{2,3,1,0:T(8,128)S(1)}, f32[5,1,1,128]{2,3,1,0:T(8,128)S(1)}, u32[]{:S(2)}, u32[]{:S(2)}) %collective-permute-start) | collective-permute-done | bytes 2592 | tf_op jit(solution)/shard_map/ppermute | solution.py:41
  18.7 0.7 %broadcast_select_fusion.3 = (f32[1,256,128]{1,2,0:T(8,128)S(1)}, f32[1,256,128]{1,2,0:T(8,128)}, f32[1,1,256,128]{2,3,1,0:T(8,128)S(1)}) fusion(pred[256]{0:T(512)(128)(4,1)S(1)} %iota_compare_fusion.2, f32[1,256,128]{1,2,0:T(8,128)S(1)} %get-tuple-element.155, f32[1,256,128]{1,2,0:T(8,128)S(1)} %get-tuple-element.69), kind=kLoop, calls=%fused_computation.163 | loop fusion | flops 131072 | bytes 655616 | tf_op jit(solution)/shard_map/jit(_where)/select_n | solution.py:110
  28.6 0.3 collective-permute-start.4
  29.0 0.7 %pad_maximum_fusion.16 = (f32[5,1,258,1]{2,3,1,0:T(1,128)}, f32[5,1,258,1]{2,3,1,0:T(1,128)}) fusion(f32[5,1,1,128]{2,3,1,0:T(8,128)S(1)} %collective-permute-done.1, f32[5,1,256,128]{2,3,1,0:T(8,128)S(1)} %select_select_fusion, f32[5,1,1,128]{2,3,1,0:T(8,128)S(1)} %collective-permute-done), kind=kLoop, calls=%fused_computation.259 | loop fusion | flops 5160 | bytes 670800 | tf_op jit(solution)/shard_map/slice | solution.py:38
  29.8 1.6 %collective-permute-start.3 = (f32[5,1,258,1]{2,3,1,0:T(1,128)}, f32[5,1,258,1]{2,3,1,0:T(1,128)S(1)}, u32[]{:S(2)}, u32[]{:S(2)}) collective-permute-start(f32[5,1,258,1]{2,3,1,0:T(1,128)} %get-tuple-element.113), channel_id=1, source_target_pairs={{1,0},{0,1},{3,2},{2,3},{5,4},{4,5},{7,6},{6,7},{9,8},{8,9},{11,10... | collective-permute-start | bytes 15488 | tf_op jit(solution)/shard_map/ppermute | solution.py:43
  31.4 0.5 collective-permute-start.2
  32.0 0.7 %copy.137 = f32[3,1,1,128]{3,2,1,0:T(1,128)} copy(f32[3,1,1,128]{2,3,1,0:T(8,128)S(1)} %slice.1175) | data formatting | bytes 3072 | tf_op jit(solution)/shard_map/slice | solution.py:122
  32.8 0.8 %collective-permute-done.4 = f32[5,1,1,128]{2,3,1,0:T(8,128)S(1)} collective-permute-done((f32[5,1,1,128]{2,3,1,0:T(8,128)S(1)}, f32[5,1,1,128]{2,3,1,0:T(8,128)S(1)}, u32[]{:S(2)}, u32[]{:S(2)}) %collective-permute-start.4) | collective-permute-done | bytes 2592 | tf_op jit(solution)/shard_map/ppermute | solution.py:31
  33.7 0.8 %copy-done.1 = f32[1,256,128]{1,2,0:T(8,128)S(1)} copy-done((f32[1,256,128]{1,2,0:T(8,128)S(1)}, f32[1,256,128]{1,2,0:T(8,128)}, u32[]{:S(2)}) %copy-start.1) | copy-done | bytes 131096
  34.8 0.7 %copy-done.2 = f32[3,1,1,128]{3,2,1,0:T(1,128)S(1)} copy-done((f32[3,1,1,128]{3,2,1,0:T(1,128)S(1)}, f32[3,1,1,128]{3,2,1,0:T(1,128)}, u32[]{:S(2)}) %copy-start.2) | copy-done | bytes 1560
  35.8 0.6 copy-done.3
  36.6 0.6 copy-done.8
  37.4 0.6 copy-done.6
  39.9 3.6 %collective-permute-done.6 = f32[2,6,1,1,128]{4,2,3,1,0:T(1,128)S(1)} collective-permute-done((f32[2,6,1,1,128]{4,2,3,1,0:T(1,128)S(1)}, f32[2,6,1,1,128]{4,2,3,1,0:T(1,128)S(1)}, u32[]{:S(2)}, u32[]{:S(2)}) %collective-permute-start.6) | collective-permute-done | bytes 6176 | tf_op jit(solution)/shard_map/ppermute | solution.py:18
  43.8 3.5 %collective-permute-done.7 = f32[4,6,1,1,128]{4,2,3,1,0:T(1,128)S(1)} collective-permute-done((f32[4,6,1,1,128]{4,2,3,1,0:T(1,128)S(1)}, f32[4,6,1,1,128]{4,2,3,1,0:T(1,128)S(1)}, u32[]{:S(2)}, u32[]{:S(2)}) %collective-permute-start.7) | collective-permute-done | bytes 12320 | tf_op jit(solution)/shard_map/ppermute | solution.py:18
  47.4 2.1 %collective-permute-start.8 = (f32[8,6,1,1,128]{4,0,1,3,2:T(8,128)S(1)}, f32[8,6,1,1,128]{4,0,1,3,2:T(8,128)S(1)}, u32[]{:S(2)}, u32[]{:S(2)}) collective-permute-start(f32[8,6,1,1,128]{4,0,1,3,2:T(8,128)S(1)} %copy.141), channel_id=1, source_target_pairs={{0,16},{2,18},{4,20},{6,22},{8,24},{10,26},{12,28},{14,30},{16,0},... | collective-permute-start | bytes 73736 | tf_op jit(solution)/shard_map/ppermute | solution.py:18
  49.5 2.6 %collective-permute-done.8 = f32[8,6,1,1,128]{4,0,1,3,2:T(8,128)S(1)} collective-permute-done((f32[8,6,1,1,128]{4,0,1,3,2:T(8,128)S(1)}, f32[8,6,1,1,128]{4,0,1,3,2:T(8,128)S(1)}, u32[]{:S(2)}, u32[]{:S(2)}) %collective-permute-start.8) | collective-permute-done | bytes 24608 | tf_op jit(solution)/shard_map/ppermute | solution.py:18
  52.9 0.7 %copy-done.5 = pred[256]{0:T(512)(128)(4,1)S(1)} copy-done((pred[256]{0:T(512)(128)(4,1)S(1)}, pred[256]{0:T(512)(128)(4,1)}, u32[]{:S(2)}) %copy-start.5) | copy-done | bytes 280
  55.6 1.6 %collective-permute-start.9 = (f32[5,1,256,1]{2,3,1,0:T(1,128)S(1)}, f32[5,1,256,1]{2,3,1,0:T(1,128)S(1)}, u32[]{:S(2)}, u32[]{:S(2)}) collective-permute-start(f32[5,1,256,1]{2,3,1,0:T(1,128)S(1)} %slice.1306), channel_id=1, source_target_pairs={{0,1},{1,0},{2,3},{3,2},{4,5},{5,4},{6,7},{7,6},{8,9},{9,8},{10,11... | collective-permute-start | bytes 15368 | tf_op jit(solution)/shard_map/ppermute | solution.py:31
  57.2 2.1 %collective-permute-done.9 = f32[5,1,256,1]{2,3,1,0:T(1,128)S(1)} collective-permute-done((f32[5,1,256,1]{2,3,1,0:T(1,128)S(1)}, f32[5,1,256,1]{2,3,1,0:T(1,128)S(1)}, u32[]{:S(2)}, u32[]{:S(2)}) %collective-permute-start.9) | collective-permute-done | bytes 5152 | tf_op jit(solution)/shard_map/ppermute | solution.py:31
  59.3 4.4 %all_gather.3 = f32[6,1,256,2]{2,1,0,3:T(1,128)S(1)} all-gather(f32[6,1,256,1]{2,1,0,3:T(1,128)S(1)} %maximum_bitcast_fusion.4), channel_id=1, replica_groups=mesh['gx'=16,'gy'=2] {'gy'}, dimensions={3}, use_global_device_ids=true | all-gather | bytes 18432 | tf_op jit(solution)/shard_map/all_gather | solution.py:150
  63.9 0.9 %copy.147 = f32[3,1,256,128]{3,2,1,0:T(8,128)} copy(f32[3,1,256,128]{2,3,1,0:T(8,128)S(1)} %fusion.1) | data formatting | bytes 786432 | tf_op jit(solution)/shard_map/jit(_where)/select_n | solution.py:127
  (247 shorter events, 16.6 us)
Async XLA Ops:
  3.4 8.5 %copy-start = (f32[3,1,256,128]{3,2,1,0:T(8,128)S(1)}, f32[3,1,256,128]{3,2,1,0:T(8,128)}, u32[]{:S(2)}) copy-start(f32[3,1,256,128]{3,2,1,0:T(8,128)} %param.4) | copy-start | bytes 1179652
  3.6 10.1 %collective-permute-start.1 = (f32[5,1,1,128]{2,3,1,0:T(8,128)S(1)}, f32[5,1,1,128]{2,3,1,0:T(8,128)S(1)}, u32[]{:S(2)}, u32[]{:S(2)}) collective-permute-start(f32[5,1,1,128]{2,3,1,0:T(8,128)S(1)} %get-tuple-element.151), channel_id=1, source_target_pairs={{2,0},{4,2},{6,4},{8,6},{10,8},{12,10},{14,12},{16,14},{18,16},{20... | collective-permute-start | bytes 7688 | tf_op jit(solution)/shard_map/ppermute | solution.py:43
  9.0 9.2 %collective-permute-start = (f32[5,1,1,128]{2,3,1,0:T(8,128)S(1)}, f32[5,1,1,128]{2,3,1,0:T(8,128)S(1)}, u32[]{:S(2)}, u32[]{:S(2)}) collective-permute-start(f32[5,1,1,128]{2,3,1,0:T(8,128)S(1)} %get-tuple-element.150), channel_id=1, source_target_pairs={{0,2},{2,4},{4,6},{6,8},{8,10},{10,12},{12,14},{14,16},{16,18},{18... | collective-permute-start | bytes 7688 | tf_op jit(solution)/shard_map/ppermute | solution.py:41
  11.8 7.9 %copy-start.4 = (pred[256]{0:T(512)(128)(4,1)}, pred[256]{0:T(512)(128)(4,1)S(1)}, u32[]{:S(2)}) copy-start(pred[256]{0:T(512)(128)(4,1)S(1)} %iota_compare_fusion.2) | copy-start | bytes 772
  28.6 4.9 %collective-permute-start.4 = (f32[5,1,1,128]{2,3,1,0:T(8,128)S(1)}, f32[5,1,1,128]{2,3,1,0:T(8,128)S(1)}, u32[]{:S(2)}, u32[]{:S(2)}) collective-permute-start(f32[5,1,1,128]{2,3,1,0:T(8,128)S(1)} %slice.1172), channel_id=1, source_target_pairs={{0,30},{2,0},{4,2},{6,4},{8,6},{10,8},{12,10},{14,12},{16,14},{18,... | collective-permute-start | bytes 7688 | tf_op jit(solution)/shard_map/ppermute | solution.py:31
  29.8 5.8 %collective-permute-start.3 = (f32[5,1,258,1]{2,3,1,0:T(1,128)}, f32[5,1,258,1]{2,3,1,0:T(1,128)S(1)}, u32[]{:S(2)}, u32[]{:S(2)}) collective-permute-start(f32[5,1,258,1]{2,3,1,0:T(1,128)} %get-tuple-element.113), channel_id=1, source_target_pairs={{1,0},{0,1},{3,2},{2,3},{5,4},{4,5},{7,6},{6,7},{9,8},{8,9},{11,10... | collective-permute-start | bytes 15488 | tf_op jit(solution)/shard_map/ppermute | solution.py:43
  31.4 4.2 %collective-permute-start.2 = (f32[5,1,258,1]{2,3,1,0:T(1,128)}, f32[5,1,258,1]{2,3,1,0:T(1,128)S(1)}, u32[]{:S(2)}, u32[]{:S(2)}) collective-permute-start(f32[5,1,258,1]{2,3,1,0:T(1,128)} %get-tuple-element.112), channel_id=1, source_target_pairs={{0,1},{1,0},{2,3},{3,2},{4,5},{5,4},{6,7},{7,6},{8,9},{9,8},{10,11... | collective-permute-start | bytes 15488 | tf_op jit(solution)/shard_map/ppermute | solution.py:41
  33.6 0.9 %copy-start.1 = (f32[1,256,128]{1,2,0:T(8,128)S(1)}, f32[1,256,128]{1,2,0:T(8,128)}, u32[]{:S(2)}) copy-start(f32[1,256,128]{1,2,0:T(8,128)} %get-tuple-element.103) | copy-start | bytes 393220
  34.8 0.7 %copy-start.2 = (f32[3,1,1,128]{3,2,1,0:T(1,128)S(1)}, f32[3,1,1,128]{3,2,1,0:T(1,128)}, u32[]{:S(2)}) copy-start(f32[3,1,1,128]{3,2,1,0:T(1,128)} %copy.137) | copy-start | bytes 4612
  35.5 4.3 %collective-permute-start.5 = (f32[1,6,1,1,128]{4,0,3,2,1:T(1,128)S(1)}, f32[1,6,1,1,128]{4,0,3,2,1:T(1,128)S(1)}, u32[]{:S(2)}, u32[]{:S(2)}) collective-permute-start(f32[1,6,1,1,128]{4,0,3,2,1:T(1,128)S(1)} %fusion.191), channel_id=1, source_target_pairs={{0,2},{2,0},{4,6},{6,4},{8,10},{10,8},{12,14},{14,12},{16,18},{18,... | collective-permute-start | bytes 9224 | tf_op jit(solution)/shard_map/ppermute | solution.py:18
  35.8 0.7 %copy-start.3 = (pred[128]{0:T(512)(128)(4,1)S(1)}, pred[128]{0:T(512)(128)(4,1)}, u32[]{:S(2)}) copy-start(pred[128]{0:T(512)(128)(4,1)} %iota_compare_fusion.5) | copy-start | bytes 388
  36.6 0.7 %copy-start.8 = (pred[128]{0:T(512)(128)(4,1)S(1)}, pred[128]{0:T(512)(128)(4,1)}, u32[]{:S(2)}) copy-start(pred[128]{0:T(512)(128)(4,1)} %fusion.78) | copy-start | bytes 388
  36.6 0.7 %copy-start.9 = (pred[128]{0:T(512)(128)(4,1)S(1)}, pred[128]{0:T(512)(128)(4,1)}, u32[]{:S(2)}) copy-start(pred[128]{0:T(512)(128)(4,1)} %iota_compare_fusion.4) | copy-start | bytes 388
  37.4 0.7 %copy-start.6 = (pred[128]{0:T(512)(128)(4,1)S(1)}, pred[128]{0:T(512)(128)(4,1)}, u32[]{:S(2)}) copy-start(pred[128]{0:T(512)(128)(4,1)} %fusion.77) | copy-start | bytes 388
  37.4 0.7 %copy-start.7 = (pred[128]{0:T(512)(128)(4,1)S(1)}, pred[128]{0:T(512)(128)(4,1)}, u32[]{:S(2)}) copy-start(pred[128]{0:T(512)(128)(4,1)} %iota_compare_fusion.3) | copy-start | bytes 388
  39.8 3.7 %collective-permute-start.6 = (f32[2,6,1,1,128]{4,2,3,1,0:T(1,128)S(1)}, f32[2,6,1,1,128]{4,2,3,1,0:T(1,128)S(1)}, u32[]{:S(2)}, u32[]{:S(2)}) collective-permute-start(f32[2,6,1,1,128]{4,2,3,1,0:T(1,128)S(1)} %get-tuple-element.376), channel_id=1, source_target_pairs={{0,4},{2,6},{4,0},{6,2},{8,12},{10,14},{12,8},{14,10},{16,20},{18,... | collective-permute-start | bytes 18440 | tf_op jit(solution)/shard_map/ppermute | solution.py:18
  43.5 3.8 %collective-permute-start.7 = (f32[4,6,1,1,128]{4,2,3,1,0:T(1,128)S(1)}, f32[4,6,1,1,128]{4,2,3,1,0:T(1,128)S(1)}, u32[]{:S(2)}, u32[]{:S(2)}) collective-permute-start(f32[4,6,1,1,128]{4,2,3,1,0:T(1,128)S(1)} %bitcast.368), channel_id=1, source_target_pairs={{0,8},{2,10},{4,12},{6,14},{8,0},{10,2},{12,4},{14,6},{16,24},{18,... | collective-permute-start | bytes 36872 | tf_op jit(solution)/shard_map/ppermute | solution.py:18
  47.4 4.8 %collective-permute-start.8 = (f32[8,6,1,1,128]{4,0,1,3,2:T(8,128)S(1)}, f32[8,6,1,1,128]{4,0,1,3,2:T(8,128)S(1)}, u32[]{:S(2)}, u32[]{:S(2)}) collective-permute-start(f32[8,6,1,1,128]{4,0,1,3,2:T(8,128)S(1)} %copy.141), channel_id=1, source_target_pairs={{0,16},{2,18},{4,20},{6,22},{8,24},{10,26},{12,28},{14,30},{16,0},... | collective-permute-start | bytes 73736 | tf_op jit(solution)/shard_map/ppermute | solution.py:18
  52.9 0.7 %copy-start.5 = (pred[256]{0:T(512)(128)(4,1)S(1)}, pred[256]{0:T(512)(128)(4,1)}, u32[]{:S(2)}) copy-start(pred[256]{0:T(512)(128)(4,1)} %copy-done.4) | copy-start | bytes 772
  55.6 3.7 %collective-permute-start.9 = (f32[5,1,256,1]{2,3,1,0:T(1,128)S(1)}, f32[5,1,256,1]{2,3,1,0:T(1,128)S(1)}, u32[]{:S(2)}, u32[]{:S(2)}) collective-permute-start(f32[5,1,256,1]{2,3,1,0:T(1,128)S(1)} %slice.1306), channel_id=1, source_target_pairs={{0,1},{1,0},{2,3},{3,2},{4,5},{5,4},{6,7},{7,6},{8,9},{9,8},{10,11... | collective-permute-start | bytes 15368 | tf_op jit(solution)/shard_map/ppermute | solution.py:31
